TPU v7x, 1024 devices: a whole 4x4x32 slice. The times are simulated.
1024 devices in a mesh: expert: 16 (over z_hi, y), dp: 64 (over x, z_lo, core).
Axes of the slice: x: 4, y: 4, z: 32 (z_hi: 4, z_lo: 8; z = z_hi * 8 + z_lo), core: 2. Of those that a mesh axis runs over, the one named last changes fastest.
Arguments:
- tokens: bfloat16 [262144, 512], P(('expert', 'dp')), may hold values from -6 to 6
- cotangent: bfloat16 [262144, 512], P(('expert', 'dp')), may hold values from -6 to 6
- gates: float32 [262144], P(('expert', 'dp')), may hold values from 0.1 to 1
- expert_ids: int32 [262144], P(('expert', 'dp')), may hold values from 0 to 31
- slot_ids: int32 [262144], P(('expert', 'dp')), may hold values from -1 to 9, as said below
- w_in: bfloat16 [32, 512, 1024], P('expert'), may hold values from -0.25 to 0.25
- w_out: bfloat16 [32, 1024, 512], P('expert'), may hold values from -0.1875 to 0.1875
Outputs:
- grad_tokens: bfloat16 [262144, 512], P(('expert', 'dp'))
- grad_w_out: float32 [1024, 32, 512], P('dp', 'expert')
Inputs may be any that keep to these rules, and one draw needn't show every extreme that they name: slot_ids[t] is the number of earlier tokens of t's group with t's expert if that is under 10, else -1; in every group some expert fills all 10 slots and drops tokens.
All inputs are finite; a program needn't handle non-finite values.
Results may differ from a plain program's by a relative error of at most 0.0057.
Values may be sent and summed in bfloat16 or wider, within the bound.
A program may use at most 32 MiB of HBM per device.

v0:
```python
import math

import jax
import jax.numpy as jnp
from jax import lax
from jax.sharding import PartitionSpec as P

GROUP = 256


def on_device(tokens, cotangent, gates, expert_ids, slot_ids, w_in, w_out):
    tok_rows, width = tokens.shape
    groups = tok_rows // GROUP
    n_expert = lax.axis_size("expert")
    n_replica = lax.axis_size("dp")
    local_exp = w_in.shape[0]
    all_exp = local_exp * n_expert
    capacity = (5 * GROUP + 4 * all_exp - 1) // (4 * all_exp)
    weight_scale = 1.0 / math.sqrt(groups * n_expert * n_replica * capacity)
    e_match = (
        expert_ids.reshape(groups, GROUP)[:, :, None]
        == jnp.arange(all_exp, dtype=jnp.int32)[None, None, :]
    )
    c_match = (
        slot_ids.reshape(groups, GROUP)[:, :, None]
        == jnp.arange(capacity, dtype=jnp.int32)[None, None, :]
    )
    table = (
        (e_match[:, :, :, None] & c_match[:, :, None, :])
        .reshape(groups, GROUP, all_exp * capacity)
        .astype(jnp.bfloat16)
    )
    scaled = (cotangent.astype(jnp.float32) * gates[:, None]).astype(jnp.bfloat16)
    x_buf = jnp.einsum(
        "gtk,gtd->kgd",
        table,
        tokens.reshape(groups, GROUP, width),
        preferred_element_type=jnp.float32,
    )
    x_buf = x_buf.astype(jnp.bfloat16).reshape(all_exp, capacity * groups, width)
    g_buf = jnp.einsum(
        "gtk,gtd->kgd",
        table,
        scaled.reshape(groups, GROUP, width),
        preferred_element_type=jnp.float32,
    )
    g_buf = g_buf.astype(jnp.bfloat16).reshape(all_exp, capacity * groups, width)
    x_rows, g_rows = (
        lax.all_to_all(x_buf, "expert", split_axis=0, concat_axis=1, tiled=True),
        lax.all_to_all(g_buf, "expert", split_axis=0, concat_axis=1, tiled=True),
    )
    pre = jnp.einsum("erd,edf->erf", x_rows, w_in, preferred_element_type=jnp.float32)
    hidden, pull = jax.vjp(jax.nn.gelu, pre)
    hidden_b = hidden.astype(jnp.bfloat16)
    grad_hidden = jnp.einsum("erd,efd->erf", g_rows, w_out, preferred_element_type=jnp.float32)
    grad_pre = pull(grad_hidden)[0].astype(jnp.bfloat16)
    grad_rows = jnp.einsum(
        "erf,edf->erd", grad_pre, w_in, preferred_element_type=jnp.float32
    ).astype(jnp.bfloat16)
    back = lax.all_to_all(grad_rows, "expert", split_axis=1, concat_axis=0, tiled=True)
    back = back.reshape(all_exp * capacity, groups, width)
    grad_tokens = jnp.einsum("gtk,kgd->gtd", table, back, preferred_element_type=jnp.float32)
    grad_tokens = grad_tokens.astype(jnp.bfloat16).reshape(tok_rows, width)
    term = (
        jnp.einsum("erf,erd->fed", hidden_b, g_rows, preferred_element_type=jnp.float32)
        * weight_scale
    )
    grad_w_out = lax.psum_scatter(term, "dp", scatter_dimension=0, tiled=True)
    return (grad_tokens, grad_w_out)


def solution(mesh):
    return jax.shard_map(
        on_device,
        mesh=mesh,
        in_specs=(
            P(("expert", "dp"), None),
            P(("expert", "dp"), None),
            P(("expert", "dp")),
            P(("expert", "dp")),
            P(("expert", "dp")),
            P("expert", None, None),
            P("expert", None, None),
        ),
        out_specs=(P(("expert", "dp"), None), P("dp", "expert", None)),
        check_vma=False,
    )
```

profile of v0, /device:TPU:1, one launch (start us, length us, event | category | flops | bytes accessed | tf_op | source)
XLA Modules:
  0.0 1050.4 jit_solution(15902278796283696952)
XLA Ops:
  7.2 0.0 copy-start
  7.2 0.8 iota_compare_fusion
  8.0 0.7 iota_compare_fusion.1
  8.7 0.1 broadcast_and_fusion
  8.8 0.1 and.33
  8.9 0.0 copy-start.2
  8.9 0.0 copy-start.3
  8.9 1.2 fusion.8
  10.1 0.9 reshape.111
  11.0 31.6 %all-to-all-start.1 = ((bf16[32,10,512]{2,1,0:T(8,128)(2,1)}), bf16[32,10,512]{2,1,0:T(8,128)(2,1)S(1)}, u32[]{:S(2)}, u32[]{:S(2)}) async-start(bf16[32,10,512]{2,1,0:T(8,128)(2,1)} %reshape.111), calls=%async_computation.1 | async-start | bytes 1048576 | tf_op jit(solution)/shard_map/all_to_all | solution.py:49
  42.7 0.0 copy-done.2
  42.7 0.0 copy-done.3
  42.7 0.3 fusion.7
  43.0 0.9 reshape.110
  43.9 39.7 %all-to-all-done.1 = bf16[32,10,512]{2,1,0:T(8,128)(2,1)S(1)} async-done(((bf16[32,10,512]{2,1,0:T(8,128)(2,1)}), bf16[32,10,512]{2,1,0:T(8,128)(2,1)S(1)}, u32[]{:S(2)}, u32[]{:S(2)}) %all-to-all-start.1) | async-done | bytes 327712 | tf_op jit(solution)/shard_map/all_to_all | solution.py:49
  83.6 28.7 %all-to-all-start = ((bf16[32,10,512]{2,1,0:T(8,128)(2,1)}), bf16[32,10,512]{2,1,0:T(8,128)(2,1)S(1)}, u32[]{:S(2)}, u32[]{:S(2)}) async-start(bf16[32,10,512]{2,1,0:T(8,128)(2,1)} %reshape.110), calls=%async_computation | async-start | bytes 1048576 | tf_op jit(solution)/shard_map/all_to_all | solution.py:50
  112.3 0.0 all-reduce.3.cloned.1.call-start
  112.3 1.1 copy.22
  113.4 56.0 %all-to-all-done = bf16[32,10,512]{2,1,0:T(8,128)(2,1)S(1)} async-done(((bf16[32,10,512]{2,1,0:T(8,128)(2,1)}), bf16[32,10,512]{2,1,0:T(8,128)(2,1)S(1)}, u32[]{:S(2)}, u32[]{:S(2)}) %all-to-all-start) | async-done | bytes 327712 | tf_op jit(solution)/shard_map/all_to_all | solution.py:50
  169.5 0.3 copy.20
  169.8 0.0 copy-start.1
  169.8 0.0 copy-done
  169.8 1.6 fusion.14
  171.4 0.0 copy-done.1
  171.4 2.8 multiply_bitcast_fusion
  174.2 7.2 copy.27
  181.5 0.0 all-reduce.3.cloned.1.call-update
  181.5 4.4 convolution_convert_fusion.2
  185.9 2.1 copy.24
  187.9 9.9 all-to-all-start.2
  197.8 1.3 dynamic-slice
  199.8 24.6 %all-to-all-done.2 = bf16[2,160,512]{2,0,1:T(2,128)(2,1)S(1)} async-done(((bf16[2,160,512]{2,0,1:T(2,128)(2,1)}), bf16[2,160,512]{2,0,1:T(2,128)(2,1)S(1)}, u32[]{:S(2)}, u32[]{:S(2)}) %all-to-all-start.2) | async-done | bytes 327712 | tf_op jit(solution)/shard_map/all_to_all | solution.py:60
  224.4 0.1 copy.25
  224.5 0.1 reshape.112
  224.6 1.1 convolution_convert_fusion.3
  225.6 816.4 %all-reduce.3.cloned.1.call-done = f32[1024,2,512]{2,1,0:T(2,128)} async-done(((f32[1024,2,512]{2,1,0:T(2,128)}), f32[1024,2,512]{2,1,0:T(2,128)}) %all-reduce.3.cloned.1.call-update) | async-done | bytes 4194320
  1042.1 1.5 constant_dynamic-slice_fusion
Async XLA Ops:
  7.2 162.6 %copy-start = (bf16[2,512,1024]{2,1,0:T(8,128)(2,1)S(1)}, bf16[2,512,1024]{2,1,0:T(8,128)(2,1)}, u32[]{:S(2)}) copy-start(bf16[2,512,1024]{2,1,0:T(8,128)(2,1)} %param.12) | copy-start | bytes 6291460
  8.9 33.8 %copy-start.2 = (bf16[256,512]{1,0:T(8,128)(2,1)S(1)}, bf16[256,512]{1,0:T(8,128)(2,1)}, u32[]{:S(2)}) copy-start(bf16[256,512]{1,0:T(8,128)(2,1)} %param.8) | copy-start | bytes 786436
  8.9 33.8 %copy-start.3 = (f32[256]{0:T(256)S(1)}, f32[256]{0:T(256)}, u32[]{:S(2)}) copy-start(f32[256]{0:T(256)} %param.9) | copy-start | bytes 3076
  11.0 72.6 %all-to-all-start.1 = ((bf16[32,10,512]{2,1,0:T(8,128)(2,1)}), bf16[32,10,512]{2,1,0:T(8,128)(2,1)S(1)}, u32[]{:S(2)}, u32[]{:S(2)}) async-start(bf16[32,10,512]{2,1,0:T(8,128)(2,1)} %reshape.111), calls=%async_computation.1 | async-start | bytes 1048576 | tf_op jit(solution)/shard_map/all_to_all | solution.py:49
  83.6 85.8 %all-to-all-start = ((bf16[32,10,512]{2,1,0:T(8,128)(2,1)}), bf16[32,10,512]{2,1,0:T(8,128)(2,1)S(1)}, u32[]{:S(2)}, u32[]{:S(2)}) async-start(bf16[32,10,512]{2,1,0:T(8,128)(2,1)} %reshape.110), calls=%async_computation | async-start | bytes 1048576 | tf_op jit(solution)/shard_map/all_to_all | solution.py:50
  112.3 929.8 %all-reduce.3.cloned.1.call-start = ((), (), s32[]{:S(2)}) async-start(), calls=%async_computation.3 | async-start | bytes 8388608
  169.8 1.6 copy-start.1
  187.9 36.4 %all-to-all-start.2 = ((bf16[2,160,512]{2,0,1:T(2,128)(2,1)}), bf16[2,160,512]{2,0,1:T(2,128)(2,1)S(1)}, u32[]{:S(2)}, u32[]{:S(2)}) async-start(bf16[2,160,512]{2,0,1:T(2,128)(2,1)} %copy.24), calls=%async_computation.2 | async-start | bytes 655360 | tf_op jit(solution)/shard_map/all_to_all | solution.py:60
Sparse Core Ops, SparseCore 0:
  181.6 860.3 all-reduce.2
where the time goes:
time: 1050 us
  waiting for transfers between devices  937 us (89%)
  starting transfers between devices  70.2 us (7%)
  local copies, waits for them, and re-layouts  15.6 us (1%)
  between operations  14.8 us (1%)
  matrix products  11.4 us (1%)
    unnamed x2, waiting for transfers between devices  816 us
    all_to_all x1, waiting for transfers between devices, on_device(): lax.all_to_all(g_buf, 'expert', split_axis=0, concat_axis=1, tiled=True)  56 us
    all_to_all x1, waiting for transfers between devices, on_device(): lax.all_to_all(x_buf, 'expert', split_axis=0, concat_axis=1, tiled=True)  39.7 us
    all_to_all x1, starting transfers between devices, on_device(): lax.all_to_all(x_buf, 'expert', split_axis=0, concat_axis=1, tiled=True)  31.6 us
    all_to_all x1, starting transfers between devices, on_device(): lax.all_to_all(g_buf, 'expert', split_axis=0, concat_axis=1, tiled=True)  28.7 us
    all_to_all x1, waiting for transfers between devices, on_device(): lax.all_to_all(grad_rows, 'expert', split_axis=1, concat_axis=0, tiled=True)  24.6 us
  transfers between devices with their start and end apart: 4, of which 4 were waited for; matrix products, arithmetic and copies ran while one was open for 1% of the time, Pallas kernels for 0%

commit v1 on v0

v1 whole, which is shorter than its diff:
```python
import functools
import math

import jax
import jax.numpy as jnp
from jax import lax
from jax.experimental import pallas as pl
from jax.experimental.pallas import tpu as pltpu
from jax.sharding import PartitionSpec as P

MESH = pl.DeviceIdType.MESH
CAP = 10
F32 = jnp.float32
BF16 = jnp.bfloat16
ZH, Y, X, ZL, C = 4, 4, 4, 8, 2


def nn(a, b):
    return lax.dot_general(a, b, (((1,), (0,)), ((), ())), preferred_element_type=F32)


def nt(a, b):
    return lax.dot_general(a, b, (((1,), (1,)), ((), ())), preferred_element_type=F32)


def tn(a, b):
    return lax.dot_general(a, b, (((0,), (0,)), ((), ())), preferred_element_type=F32)


def one_hot(rows, cols):
    return jnp.where(rows == cols, 1.0, 0.0).astype(BF16)


def kernel(
    dims, scale,
    tok_hbm, cot_hbm, gate_ref, eid_ref, sid_ref, win_hbm, wout_hbm,
    gt_ref, gw_ref,
    tok, cot, win, wout, send, recv, xg32, xg, grow, sback, rback,
    own, csend, crecv, xsend, xrecv, zsend, zrecv,
    in_sem, w_sem, fs, fr, bs, br, cs, cr, xs, xr, zs, zr,
):
    zh_n, y_n, x_n, zl_n, c_n = dims
    n = zh_n * y_n
    tokens, width = tok.shape
    ff = win.shape[2]
    half = width // 2
    quarter = width // 4
    chunk = ff // x_n
    main = 16 * n

    ex = lax.axis_index("expert")
    dp = lax.axis_index("dp")
    zh, yy = ex // y_n, ex % y_n
    xx, zl, core = dp // (zl_n * c_n), (dp // c_n) % zl_n, dp % c_n

    def expert_peer(k):
        to_z = (zh + k // y_n) % zh_n
        to_y = (yy + k % y_n) % y_n
        return to_z * y_n + to_y

    def dp_id(a, b, c):
        return (a * zl_n + b) * c_n + c

    in_copies = [
        pltpu.make_async_copy(tok_hbm, tok, in_sem.at[0]),
        pltpu.make_async_copy(cot_hbm, cot, in_sem.at[1]),
    ]
    w_copies = [
        pltpu.make_async_copy(win_hbm, win, w_sem.at[0]),
        pltpu.make_async_copy(wout_hbm, wout, w_sem.at[1]),
    ]
    for copy in in_copies + w_copies:
        copy.start()

    barrier = pltpu.get_barrier_semaphore()

    def greet(to_e, to_d):
        pl.semaphore_signal(barrier, inc=1, device_id=(to_e, to_d), device_id_type=MESH)

    def greet_expert(k, carry):
        greet(expert_peer(k), dp)
        return carry

    lax.fori_loop(1, n, greet_expert, 0)
    greet(ex, dp_id(xx, zl, 1 - core))
    for k in range(1, x_n):
        greet(ex, dp_id((xx + k) % x_n, zl, core))
    for k in range(1, zl_n):
        greet(ex, dp_id(xx, (zl + k) % zl_n, core))

    slot = sid_ref[...]
    code = jnp.where(slot >= 0, eid_ref[...] * CAP + slot, -1)
    row = lax.broadcasted_iota(jnp.int32, (main, 1), 0)
    main_code = (row // 8) * CAP + row % 8
    tail_block = (row // 4) % 4
    tail_code = (2 * (row // 16) + (row // 2) % 2) * CAP + 8 + row % 2
    t_main = one_hot(main_code, code)
    t_tail = one_hot(tail_code, code)
    gates = gate_ref[...]
    gate_main = jnp.sum(jnp.where(main_code == code, gates, 0.0), axis=1, keepdims=True)
    gate_tail = jnp.sum(jnp.where(tail_code == code, gates, 0.0), axis=1, keepdims=True)

    for copy in in_copies:
        copy.wait()
    send[:, :, :width] = nn(t_main, tok[...]).astype(BF16).reshape(n, 16, width)
    send[:, :, width : 2 * width] = (
        (nn(t_main, cot[...]) * gate_main).astype(BF16).reshape(n, 16, width)
    )
    tail_x = nn(t_tail, tok[...])
    tail_g = nn(t_tail, cot[...]) * gate_tail
    tail = jnp.where(
        tail_block == 0,
        tail_x[:, :half],
        jnp.where(
            tail_block == 1,
            tail_x[:, half:],
            jnp.where(tail_block == 2, tail_g[:, :half], tail_g[:, half:]),
        ),
    )
    send[:, :, 2 * width :] = tail.astype(BF16).reshape(n, 16, half)

    pl.semaphore_wait(barrier, (n - 1) + 1 + (x_n - 1) + (zl_n - 1))

    def forward(to):
        return pltpu.make_async_remote_copy(
            src_ref=send.at[to], dst_ref=recv.at[ex], send_sem=fs.at[to], recv_sem=fr.at[ex],
            device_id=(to, dp), device_id_type=MESH,
        )

    def forward_from(src):
        return pltpu.make_async_remote_copy(
            src_ref=send.at[src], dst_ref=recv.at[src], send_sem=fs.at[src], recv_sem=fr.at[src],
            device_id=(src, dp), device_id_type=MESH,
        )

    def start_forward(k, carry):
        forward(expert_peer(n - k)).start()
        return carry

    lax.fori_loop(1, n, start_forward, 0)
    recv[pl.ds(ex, 1)] = send[pl.ds(ex, 1)]

    def wait_forward(k, carry):
        forward_from(expert_peer(k)).wait_recv()
        return carry

    lax.fori_loop(1, n, wait_forward, 0)

    for s in range(n):
        block = recv[s, :, : 2 * width].astype(F32)
        xg32[0, s * 8 : s * 8 + 8, :] = block[:8]
        xg32[1, s * 8 : s * 8 + 8, :] = block[8:]
    part = 2 * n
    col = lax.broadcasted_iota(jnp.int32, (1, main), 1)
    wanted = (
        ((row // 2) % n) * 16 + ((row // part) % 4) * 4 + (row // (4 * part)) * 2 + row % 2
    )
    tails = nn(one_hot(wanted, col), recv[:, :, 2 * width :].reshape(main, half))
    for a in range(2):
        for q in range(4):
            at = (a * 4 + q) * part
            xg32[a, 8 * n :, q * half : (q + 1) * half] = tails[at : at + part]
    for a in range(2):
        xg[a] = xg32[a].astype(BF16)
    for copy in w_copies:
        copy.wait()
    grow[...] = jnp.zeros_like(grow)

    other = 1 - core

    def to_core(a, to_x):
        return pltpu.make_async_remote_copy(
            src_ref=csend.at[a, to_x], dst_ref=crecv.at[a, to_x],
            send_sem=cs.at[a, to_x], recv_sem=cr.at[a, to_x],
            device_id=(ex, dp_id(xx, zl, other)), device_id_type=MESH,
        )

    k0 = 0.7978845608028654
    k1 = 0.044715

    def expert_chunk(i, carry):
        a = i % 2
        to_x = (xx + 1 + i // 2) % x_n
        f0 = pl.multiple_of(to_x * chunk, chunk)
        xa = xg[a, :, :width]
        ga = xg[a, :, width:]
        w1 = win[a, :, pl.ds(f0, chunk)]
        w2 = wout[a, pl.ds(f0, chunk), :]
        pre = nn(xa, w1)
        grad_hidden = nt(ga, w2)
        square = pre * pre
        th = jnp.tanh(k0 * pre * (1.0 + k1 * square))
        cdf = 0.5 * (1.0 + th)
        hidden = (pre * cdf).astype(BF16)
        slope = cdf + 0.5 * pre * (1.0 - th * th) * (k0 * (1.0 + 3.0 * k1 * square))
        grad_pre = (grad_hidden * slope).astype(BF16)
        grow[a] += nt(grad_pre, w1)
        term = (tn(hidden, ga) * scale).reshape(zl_n, c_n, 16, width)
        even, odd = term[:, 0], term[:, 1]
        mine = core == 0
        own[a, to_x] = jnp.where(mine, even, odd)
        csend[a, to_x] = jnp.where(mine, odd, even).astype(BF16)
        to_core(a, to_x).start()
        return carry

    lax.fori_loop(0, 2 * x_n, expert_chunk, 0)

    for s in range(n):
        both = jnp.concatenate([grow[0, s * 8 : s * 8 + 8, :], grow[1, s * 8 : s * 8 + 8, :]], axis=0)
        sback[s, :, :width] = both.astype(BF16)
    small = jnp.concatenate([grow[0, 8 * n :, :], grow[1, 8 * n :, :]], axis=0).astype(BF16)
    small_col = lax.broadcasted_iota(jnp.int32, (1, 2 * part), 1)
    spread = nn(one_hot(((row // 2) % 2) * part + (row // 16) * 2 + row % 2, small_col), small)
    cols = [spread[:, q * quarter : (q + 1) * quarter] for q in range(4)]
    picked = jnp.where(
        tail_block == 0,
        cols[0],
        jnp.where(tail_block == 1, cols[1], jnp.where(tail_block == 2, cols[2], cols[3])),
    )
    sback[:, :, width:] = picked.astype(BF16).reshape(n, 16, quarter)

    def back_to(to):
        return pltpu.make_async_remote_copy(
            src_ref=sback.at[to], dst_ref=rback.at[ex], send_sem=bs.at[to], recv_sem=br.at[ex],
            device_id=(to, dp), device_id_type=MESH,
        )

    def back_from(src):
        return pltpu.make_async_remote_copy(
            src_ref=sback.at[src], dst_ref=rback.at[src], send_sem=bs.at[src], recv_sem=br.at[src],
            device_id=(src, dp), device_id_type=MESH,
        )

    def start_back(k, carry):
        back_to(expert_peer(n - k)).start()
        return carry

    lax.fori_loop(1, n, start_back, 0)
    rback[pl.ds(ex, 1)] = sback[pl.ds(ex, 1)]

    def to_x_copy(a, to_x):
        return pltpu.make_async_remote_copy(
            src_ref=xsend.at[a, to_x], dst_ref=xrecv.at[a, xx],
            send_sem=xs.at[a, to_x], recv_sem=xr.at[a, xx],
            device_id=(ex, dp_id(to_x, zl, core)), device_id_type=MESH,
        )

    def from_x_copy(a, src):
        return pltpu.make_async_remote_copy(
            src_ref=xsend.at[a, src], dst_ref=xrecv.at[a, src],
            send_sem=xs.at[a, src], recv_sem=xr.at[a, src],
            device_id=(ex, dp_id(src, zl, core)), device_id_type=MESH,
        )

    def pass_x(i, carry):
        a = i % 2
        to_x = (xx + 1 + i // 2) % x_n
        to_core(a, to_x).wait_recv()
        xsend[a, to_x] = (own[a, to_x] + crecv[a, to_x].astype(F32)).astype(BF16)
        to_x_copy(a, to_x).start()
        return carry

    lax.fori_loop(0, 2 * (x_n - 1), pass_x, 0)
    for a in range(2):
        to_core(a, xx).wait_recv()
        own[a, xx] += crecv[a, xx].astype(F32)

    def to_z_copy(a, to_z):
        return pltpu.make_async_remote_copy(
            src_ref=zsend.at[a, to_z], dst_ref=zrecv.at[a, zl],
            send_sem=zs.at[a, to_z], recv_sem=zr.at[a, zl],
            device_id=(ex, dp_id(xx, to_z, core)), device_id_type=MESH,
        )

    def from_z_copy(a, src):
        return pltpu.make_async_remote_copy(
            src_ref=zsend.at[a, src], dst_ref=zrecv.at[a, src],
            send_sem=zs.at[a, src], recv_sem=zr.at[a, src],
            device_id=(ex, dp_id(xx, src, core)), device_id_type=MESH,
        )

    for a in range(2):
        for k in range(1, x_n):
            src = (xx + x_n - k) % x_n
            from_x_copy(a, src).wait_recv()
            own[a, xx] += xrecv[a, src].astype(F32)
        zsend[a] = own[a, xx].astype(BF16)
        for k in range(1, zl_n):
            to_z_copy(a, (zl + k) % zl_n).start()

    def wait_back(k, carry):
        back_from(expert_peer(k)).wait_recv()
        return carry

    lax.fori_loop(1, n, wait_back, 0)
    back_main = rback[:, :, :width].reshape(main, width)
    back_tail = rback[:, :, width:].reshape(main, quarter).astype(F32)
    wide = jnp.concatenate(
        [jnp.where(tail_block == q, back_tail, 0.0) for q in range(4)], axis=1
    ).astype(BF16)
    gt_ref[...] = (tn(t_main, back_main) + tn(t_tail, wide)).astype(BF16)

    for a in range(2):
        total = own[a, xx, zl]
        for k in range(1, zl_n):
            src = (zl + k) % zl_n
            from_z_copy(a, src).wait_recv()
            total = total + zrecv[a, src].astype(F32)
        gw_ref[:, a, :] = total

    def wait_sent(k, carry):
        to = expert_peer(k)
        forward(to).wait_send()
        back_to(to).wait_send()
        return carry

    lax.fori_loop(1, n, wait_sent, 0)
    for a in range(2):
        for k in range(x_n):
            to_core(a, (xx + k) % x_n).wait_send()
        for k in range(1, x_n):
            to_x_copy(a, (xx + k) % x_n).wait_send()
        for k in range(1, zl_n):
            to_z_copy(a, (zl + k) % zl_n).wait_send()


def on_device(dims, tokens, cotangent, gates, expert_ids, slot_ids, w_in, w_out):
    zh_n, y_n, x_n, zl_n, c_n = dims
    n = zh_n * y_n
    rows, width = tokens.shape
    ff = w_in.shape[2]
    scale = 1.0 / math.sqrt(n * x_n * zl_n * c_n * CAP)
    per = 10 * n
    dma = pltpu.SemaphoreType.DMA
    hbm = pl.BlockSpec(memory_space=pl.ANY)
    vmem = pl.BlockSpec(memory_space=pltpu.VMEM)
    return pl.pallas_call(
        functools.partial(kernel, dims, scale),
        out_shape=(
            jax.ShapeDtypeStruct((rows, width), BF16),
            jax.ShapeDtypeStruct((ff // (x_n * zl_n * c_n), 2, width), F32),
        ),
        in_specs=[hbm, hbm, vmem, vmem, vmem, hbm, hbm],
        out_specs=(vmem, vmem),
        scratch_shapes=[
            pltpu.VMEM((rows, width), BF16),
            pltpu.VMEM((rows, width), BF16),
            pltpu.VMEM(w_in.shape, BF16),
            pltpu.VMEM(w_out.shape, BF16),
            pltpu.VMEM((n, 16, 2 * width + width // 2), BF16),
            pltpu.VMEM((n, 16, 2 * width + width // 2), BF16),
            pltpu.VMEM((2, per, 2 * width), F32),
            pltpu.VMEM((2, per, 2 * width), BF16),
            pltpu.VMEM((2, per, width), F32),
            pltpu.VMEM((n, 16, width + width // 4), BF16),
            pltpu.VMEM((n, 16, width + width // 4), BF16),
            pltpu.VMEM((2, x_n, zl_n, 16, width), F32),
            pltpu.VMEM((2, x_n, zl_n, 16, width), BF16),
            pltpu.VMEM((2, x_n, zl_n, 16, width), BF16),
            pltpu.VMEM((2, x_n, zl_n, 16, width), BF16),
            pltpu.VMEM((2, x_n, zl_n, 16, width), BF16),
            pltpu.VMEM((2, zl_n, 16, width), BF16),
            pltpu.VMEM((2, zl_n, 16, width), BF16),
            dma((2,)),
            dma((2,)),
            dma((n,)),
            dma((n,)),
            dma((n,)),
            dma((n,)),
            dma((2, x_n)),
            dma((2, x_n)),
            dma((2, x_n)),
            dma((2, x_n)),
            dma((2, zl_n)),
            dma((2, zl_n)),
        ],
        compiler_params=pltpu.CompilerParams(
            collective_id=0, has_side_effects=True, vmem_limit_bytes=48 << 20
        ),
        cost_estimate=pl.CostEstimate(
            flops=8 * 2 * per * width * ff, bytes_accessed=6 << 20, transcendentals=2 * per * ff
        ),
        name="expert_backward",
    )(
        tokens, cotangent, gates.reshape(1, rows), expert_ids.reshape(1, rows),
        slot_ids.reshape(1, rows), w_in, w_out,
    )


def solution(mesh, dims=(ZH, Y, X, ZL, C)):
    return jax.shard_map(
        functools.partial(on_device, dims),
        mesh=mesh,
        in_specs=(
            P(("expert", "dp"), None),
            P(("expert", "dp"), None),
            P(("expert", "dp")),
            P(("expert", "dp")),
            P(("expert", "dp")),
            P("expert", None, None),
            P("expert", None, None),
        ),
        out_specs=(P(("expert", "dp"), None), P("dp", "expert", None)),
        check_vma=False,
    )
```

time: 1050 us -> 141 us (0.13)
  waiting for transfers between devices: 937 us -> 0 us
  Pallas kernels: 0 us -> 131 us
  starting transfers between devices: 70.2 us -> 0 us
  between operations: 14.8 us -> 0.66 us
  matrix products: 11.4 us -> 0 us
    unnamed x2 -> x0, waiting for transfers between devices: 816 us -> none
    pallas_call x0 -> x1, Pallas kernels: none -> 131 us  [on_device(): pl.pallas_call(functools.partial(kernel, dims, scale), out_shape=(jax.Sha...]
    all_to_all x3 -> x0, waiting for transfers between devices: 120 us -> none  [the longest x1 56 us: on_device(): lax.all_to_all(g_buf, 'expert', split_axis=0, concat_axis=1, tiled=True)]
    all_to_all x3 -> x0, starting transfers between devices: 70.2 us -> none  [the longest x1 31.6 us: on_device(): lax.all_to_all(x_buf, 'expert', split_axis=0, concat_axis=1, tiled=True)]
    dot_general x6 -> x0, matrix products: 11.4 us -> none  [the longest x1 4.35 us: on_device(): jnp.einsum('erf,edf->erd', grad_pre, w_in, preferred_element_type=jnp.flo...]
  transfers between devices with their start and end apart: 4 -> 0, of which waited for: 4 -> 0; matrix products, arithmetic and copies ran while one was open for 1% -> 0% of each run, Pallas kernels for 0% -> 0%
where the time goes in v1:
time: 141 us; the launch traced here: 140 us
  Pallas kernels  131 us (93%)
  local copies, waits for them, and re-layouts  8.44 us (6%)
    pallas_call x1, Pallas kernels, on_device(): pl.pallas_call(functools.partial(kernel, dims, scale), out_shape=(jax.Sha...  131 us
    unnamed x16, local copies, waits for them, and re-layouts  8.44 us

profile of v1, /device:TPU:1, one launch (start us, length us, event | category | flops | bytes accessed | tf_op | source)
XLA Modules:
  0.0 140.4 jit_solution(3273770560297967260)
XLA Ops:
  0.6 0.0 copy-start
  0.6 1.6 %copy-done = bf16[2,512,1024]{2,1,0:T(8,128)(2,1)S(1)} copy-done((bf16[2,512,1024]{2,1,0:T(8,128)(2,1)S(1)}, bf16[2,512,1024]{2,1,0:T(8,128)(2,1)}, u32[]{:S(2)}) %copy-start) | copy-done | bytes 2097176
  2.2 0.0 copy-start.1
  2.2 1.6 %copy-done.1 = bf16[2,1024,512]{2,1,0:T(8,128)(2,1)S(1)} copy-done((bf16[2,1024,512]{2,1,0:T(8,128)(2,1)S(1)}, bf16[2,1024,512]{2,1,0:T(8,128)(2,1)}, u32[]{:S(2)}) %copy-start.1) | copy-done | bytes 2097176
  3.8 0.0 copy-start.2
  3.8 0.9 copy-done.2
  4.8 0.0 copy-start.3
  4.8 0.9 copy-done.3
  5.7 0.0 copy-start.4
  5.7 0.7 copy-done.4
  6.4 0.0 copy-start.5
  6.4 0.7 copy-done.5
  7.1 0.0 copy-start.6
  7.1 0.7 copy-done.6
  7.8 131.3 %expert_backward.1 = (bf16[256,512]{1,0:T(8,128)(2,1)S(1)}, f32[16,2,512]{2,1,0:T(2,128)S(1)}) custom-call(bf16[256,512]{1,0:T(8,128)(2,1)S(1)} %copy-done.2, bf16[256,512]{1,0:T(8,128)(2,1)S(1)} %copy-done.3, f32[1,256]{1,0:T(1,128)S(1)} %bitcast.3, s32[1,256]{1,0:T(1,128)S(1)} %bitcast.4, s32[1,256]{1,0:T(1,128)S(1)} %bitcast.5, ...), custom_call_target="tpu_custom_call" | custom-call | flops 1342177280 | bytes 6291456 | tf_op jit(solution)/shard_map/expert_backward/pallas_call | solution.py:337
  139.0 0.7 copy.11
  139.8 0.6 copy.12
Async XLA Ops:
  0.6 1.6 %copy-start = (bf16[2,512,1024]{2,1,0:T(8,128)(2,1)S(1)}, bf16[2,512,1024]{2,1,0:T(8,128)(2,1)}, u32[]{:S(2)}) copy-start(bf16[2,512,1024]{2,1,0:T(8,128)(2,1)} %win_hbm.1) | copy-start | bytes 6291460
  2.2 1.6 %copy-start.1 = (bf16[2,1024,512]{2,1,0:T(8,128)(2,1)S(1)}, bf16[2,1024,512]{2,1,0:T(8,128)(2,1)}, u32[]{:S(2)}) copy-start(bf16[2,1024,512]{2,1,0:T(8,128)(2,1)} %wout_hbm.1) | copy-start | bytes 6291460
  3.8 0.9 copy-start.2
  4.8 0.9 copy-start.3
  5.7 0.7 copy-start.4
  6.4 0.7 copy-start.5
  7.1 0.7 copy-start.6

commit v2 on v1

v2 whole, which is shorter than its diff:
```python
import functools
import math

import jax
import jax.numpy as jnp
from jax import lax
from jax.experimental import pallas as pl
from jax.experimental.pallas import tpu as pltpu
from jax.sharding import PartitionSpec as P

MESH = pl.DeviceIdType.MESH
CAP = 10
F32 = jnp.float32
BF16 = jnp.bfloat16
ZH, Y, X, ZL, C = 4, 4, 4, 8, 2


def nn(a, b):
    return lax.dot_general(a, b, (((1,), (0,)), ((), ())), preferred_element_type=F32)


def nt(a, b):
    return lax.dot_general(a, b, (((1,), (1,)), ((), ())), preferred_element_type=F32)


def tn(a, b):
    return lax.dot_general(a, b, (((0,), (0,)), ((), ())), preferred_element_type=F32)


def one_hot(rows, cols):
    return jnp.where(rows == cols, 1.0, 0.0).astype(BF16)


def round_up(rows):
    return (rows + 15) // 16 * 16


def kernel(
    dims, scale,
    tok_hbm, cot_hbm, gate_hbm, eid_hbm, sid_hbm, win_hbm, wout_hbm,
    gt_ref, gw_ref,
    tok, cot, gate, eid, sid, win, wout, send, recv, xg_near, xg_far, tails_in, grow_near, grow_far,
    sback, rback, acc, own, csend, crecv, xsend, xrecv, zsend, zrecv,
    in_sem, w_sem, fs, fr, bs, br, cs, cr, xs, xr, zs, zr,
):
    zh_n, y_n, x_n, zl_n, c_n = dims
    n = zh_n * y_n
    tokens, width = tok.shape
    ff = win.shape[2]
    half = width // 2
    quarter = width // 4
    chunk = ff // x_n
    main = 16 * n

    ex = lax.axis_index("expert")
    dp = lax.axis_index("dp")
    zh, yy = ex // y_n, ex % y_n
    xx, zl, core = dp // (zl_n * c_n), (dp // c_n) % zl_n, dp % c_n
    other = 1 - core

    steps_z = sorted(range(zh_n), key=lambda dz: min(dz, zh_n - dz))
    offsets = [(dz, dy) for dz in steps_z for dy in range(y_n)]
    near = n - y_n

    def peer(k):
        dz, dy = offsets[k]
        return ((zh + dz) % zh_n) * y_n + (yy + dy) % y_n

    def source(k):
        dz, dy = offsets[k]
        return ((zh + zh_n - dz) % zh_n) * y_n + (yy + y_n - dy) % y_n

    def dp_id(a, b, c):
        return (a * zl_n + b) * c_n + c

    in_copies = [
        pltpu.make_async_copy(src, dst, in_sem.at[i])
        for i, (src, dst) in enumerate(
            [(eid_hbm, eid), (sid_hbm, sid), (gate_hbm, gate), (tok_hbm, tok), (cot_hbm, cot)]
        )
    ]
    w_copies = [
        pltpu.make_async_copy(win_hbm, win, w_sem.at[0]),
        pltpu.make_async_copy(wout_hbm, wout, w_sem.at[1]),
    ]
    for copy in in_copies + w_copies:
        copy.start()

    barrier = pltpu.get_barrier_semaphore()

    def greet(to_e, to_d):
        pl.semaphore_signal(barrier, inc=1, device_id=(to_e, to_d), device_id_type=MESH)

    for k in range(1, n):
        greet(peer(k), dp)
    greet(ex, dp_id(xx, zl, other))
    for k in range(1, x_n):
        greet(ex, dp_id((xx + k) % x_n, zl, core))
    for k in range(1, zl_n):
        greet(ex, dp_id(xx, (zl + k) % zl_n, core))

    for copy in in_copies[:3]:
        copy.wait()
    slot = sid[...]
    code = jnp.where(slot >= 0, eid[...] * CAP + slot, -1)
    row = lax.broadcasted_iota(jnp.int32, (main, 1), 0)
    main_code = (row // 8) * CAP + row % 8
    tail_block = (row // 4) % 4
    tail_code = (2 * (row // 16) + (row // 2) % 2) * CAP + 8 + row % 2
    t_main = one_hot(main_code, code)
    t_tail = one_hot(tail_code, code)
    gates = gate[...]
    gate_main = jnp.sum(jnp.where(main_code == code, gates, 0.0), axis=1, keepdims=True)
    gate_tail = jnp.sum(jnp.where(tail_code == code, gates, 0.0), axis=1, keepdims=True)

    for copy in in_copies[3:]:
        copy.wait()
    send[:, :, :width] = nn(t_main, tok[...]).astype(BF16).reshape(n, 16, width)
    send[:, :, width : 2 * width] = (
        (nn(t_main, cot[...]) * gate_main).astype(BF16).reshape(n, 16, width)
    )
    tail_x = nn(t_tail, tok[...])
    tail_g = nn(t_tail, cot[...]) * gate_tail
    tail = jnp.where(
        tail_block == 0,
        tail_x[:, :half],
        jnp.where(
            tail_block == 1,
            tail_x[:, half:],
            jnp.where(tail_block == 2, tail_g[:, :half], tail_g[:, half:]),
        ),
    )
    send[:, :, 2 * width :] = tail.astype(BF16).reshape(n, 16, half)

    pl.semaphore_wait(barrier, (n - 1) + 1 + (x_n - 1) + (zl_n - 1))

    def forward(to):
        return pltpu.make_async_remote_copy(
            src_ref=send.at[to], dst_ref=recv.at[ex], send_sem=fs.at[to], recv_sem=fr.at[ex],
            device_id=(to, dp), device_id_type=MESH,
        )

    def forward_from(src):
        return pltpu.make_async_remote_copy(
            src_ref=send.at[src], dst_ref=recv.at[src], send_sem=fs.at[src], recv_sem=fr.at[src],
            device_id=(src, dp), device_id_type=MESH,
        )

    def back_to(to):
        return pltpu.make_async_remote_copy(
            src_ref=sback.at[to], dst_ref=rback.at[ex], send_sem=bs.at[to], recv_sem=br.at[ex],
            device_id=(to, dp), device_id_type=MESH,
        )

    def back_from(src):
        return pltpu.make_async_remote_copy(
            src_ref=sback.at[src], dst_ref=rback.at[src], send_sem=bs.at[src], recv_sem=br.at[src],
            device_id=(src, dp), device_id_type=MESH,
        )

    for k in range(1, n):
        forward(peer(k)).start()
    recv[pl.ds(ex, 1)] = send[pl.ds(ex, 1)]

    def gather(first, count, xg):
        for k in range(count):
            src = source(first + k)
            block = recv[src, :, : 2 * width].astype(F32)
            xg[0, k * 8 : k * 8 + 8, :] = block[:8]
            xg[1, k * 8 : k * 8 + 8, :] = block[8:]
            tails_in[k * 16 : k * 16 + 16, :] = recv[src, :, 2 * width :]
        part = 2 * count
        r = lax.broadcasted_iota(jnp.int32, (8 * part, 1), 0)
        col = lax.broadcasted_iota(jnp.int32, (1, 8 * part), 1)
        wanted = (
            ((r // 2) % count) * 16
            + ((r // part) % 4) * 4
            + (r // (4 * part)) * 2
            + r % 2
        )
        tails = nn(one_hot(wanted, col), tails_in[: 8 * part, :])
        for a in range(2):
            for q in range(4):
                at = (a * 4 + q) * part
                xg[a, 8 * count : 10 * count, q * half : (q + 1) * half] = tails[at : at + part]
            spare = xg.shape[1] - 10 * count
            if spare:
                xg[a, 10 * count :, :] = jnp.zeros((spare, 2 * width), F32)

    k0 = 0.7978845608028654
    k1 = 0.044715

    def place(i):
        return i % 2, (xx + 1 + i // 2) % x_n

    def multiply(xg, grow, i):
        a, to_x = place(i)
        f0 = pl.multiple_of(to_x * chunk, chunk)
        xa = xg[a, :, :width].astype(BF16)
        ga = xg[a, :, width:].astype(BF16)
        w1 = win[a, :, pl.ds(f0, chunk)]
        w2 = wout[a, pl.ds(f0, chunk), :]
        pre = nn(xa, w1)
        grad_hidden = nt(ga, w2)
        square = pre * pre
        th = jnp.tanh(k0 * pre * (1.0 + k1 * square))
        cdf = 0.5 * (1.0 + th)
        hidden = (pre * cdf).astype(BF16)
        slope = cdf + 0.5 * pre * (1.0 - th * th) * (k0 * (1.0 + 3.0 * k1 * square))
        grad_pre = (grad_hidden * slope).astype(BF16)
        grow[a] += nt(grad_pre, w1)
        return tn(hidden, ga)

    def give_back(first, count, grow):
        for k in range(count):
            both = jnp.concatenate(
                [grow[0, k * 8 : k * 8 + 8, :], grow[1, k * 8 : k * 8 + 8, :]], axis=0
            )
            sback[source(first + k), :, :width] = both.astype(BF16)
        part = 2 * count
        small = jnp.concatenate(
            [grow[0, 8 * count : 10 * count, :], grow[1, 8 * count : 10 * count, :]], axis=0
        ).astype(BF16)
        r = lax.broadcasted_iota(jnp.int32, (16 * count, 1), 0)
        col = lax.broadcasted_iota(jnp.int32, (1, 2 * part), 1)
        spread = nn(one_hot(((r // 2) % 2) * part + (r // 16) * 2 + r % 2, col), small)
        block = (r // 4) % 4
        cols = [spread[:, q * quarter : (q + 1) * quarter] for q in range(4)]
        picked = jnp.where(
            block == 0, cols[0], jnp.where(block == 1, cols[1], jnp.where(block == 2, cols[2], cols[3]))
        ).astype(BF16)
        for k in range(count):
            sback[source(first + k), :, width:] = picked[k * 16 : k * 16 + 16]
            if first + k > 0:
                back_to(source(first + k)).start()

    for k in range(1, near):
        forward_from(source(k)).wait_recv()
    gather(0, near, xg_near)
    for copy in w_copies:
        copy.wait()
    grow_near[...] = jnp.zeros_like(grow_near)
    grow_far[...] = jnp.zeros_like(grow_far)

    def near_chunk(i, carry):
        a, to_x = place(i)
        acc[a, to_x] = multiply(xg_near, grow_near, i).reshape(zl_n, c_n, 16, width)
        return carry

    lax.fori_loop(0, 2 * x_n, near_chunk, 0)
    give_back(0, near, grow_near)
    rback[pl.ds(ex, 1)] = sback[pl.ds(ex, 1)]

    def to_core(a, to_x):
        return pltpu.make_async_remote_copy(
            src_ref=csend.at[a, to_x], dst_ref=crecv.at[a, to_x],
            send_sem=cs.at[a, to_x], recv_sem=cr.at[a, to_x],
            device_id=(ex, dp_id(xx, zl, other)), device_id_type=MESH,
        )

    def to_x_copy(a, to_x):
        return pltpu.make_async_remote_copy(
            src_ref=xsend.at[a, to_x], dst_ref=xrecv.at[a, xx],
            send_sem=xs.at[a, to_x], recv_sem=xr.at[a, xx],
            device_id=(ex, dp_id(to_x, zl, core)), device_id_type=MESH,
        )

    def from_x_copy(a, src):
        return pltpu.make_async_remote_copy(
            src_ref=xsend.at[a, src], dst_ref=xrecv.at[a, src],
            send_sem=xs.at[a, src], recv_sem=xr.at[a, src],
            device_id=(ex, dp_id(src, zl, core)), device_id_type=MESH,
        )

    def to_z_copy(a, to_z):
        return pltpu.make_async_remote_copy(
            src_ref=zsend.at[a, to_z], dst_ref=zrecv.at[a, zl],
            send_sem=zs.at[a, to_z], recv_sem=zr.at[a, zl],
            device_id=(ex, dp_id(xx, to_z, core)), device_id_type=MESH,
        )

    def from_z_copy(a, src):
        return pltpu.make_async_remote_copy(
            src_ref=zsend.at[a, src], dst_ref=zrecv.at[a, src],
            send_sem=zs.at[a, src], recv_sem=zr.at[a, src],
            device_id=(ex, dp_id(xx, src, core)), device_id_type=MESH,
        )

    def far_chunk(i):
        a, to_x = place(i)
        term = (acc[a, to_x] + multiply(xg_far, grow_far, i).reshape(zl_n, c_n, 16, width)) * scale
        even, odd = term[:, 0], term[:, 1]
        mine = core == 0
        own[a, to_x] = jnp.where(mine, even, odd)
        csend[a, to_x] = jnp.where(mine, odd, even).astype(BF16)
        to_core(a, to_x).start()

    def far_first(i, carry):
        far_chunk(i)
        return carry

    def far_next(i, carry):
        far_chunk(i)
        a, to_x = place(i - 2)
        to_core(a, to_x).wait_recv()
        xsend[a, to_x] = (own[a, to_x] + crecv[a, to_x].astype(F32)).astype(BF16)
        to_x_copy(a, to_x).start()
        return carry

    for k in range(near, n):
        forward_from(source(k)).wait_recv()
    gather(near, n - near, xg_far)
    lax.fori_loop(0, 2, far_first, 0)
    lax.fori_loop(2, 2 * x_n, far_next, 0)
    give_back(near, n - near, grow_far)

    for a in range(2):
        to_core(a, xx).wait_recv()
        own[a, xx] += crecv[a, xx].astype(F32)
    for a in range(2):
        for k in range(1, x_n):
            src = (xx + x_n - k) % x_n
            from_x_copy(a, src).wait_recv()
            own[a, xx] += xrecv[a, src].astype(F32)
        zsend[a] = own[a, xx].astype(BF16)
        for k in range(1, zl_n):
            to_z_copy(a, (zl + k) % zl_n).start()

    for k in range(1, n):
        back_from(peer(k)).wait_recv()
    back_main = rback[:, :, :width].reshape(main, width)
    back_tail = rback[:, :, width:].reshape(main, quarter).astype(F32)
    wide = jnp.concatenate(
        [jnp.where(tail_block == q, back_tail, 0.0) for q in range(4)], axis=1
    ).astype(BF16)
    gt_ref[...] = (tn(t_main, back_main) + tn(t_tail, wide)).astype(BF16)

    for a in range(2):
        total = own[a, xx, zl]
        for k in range(1, zl_n):
            src = (zl + k) % zl_n
            from_z_copy(a, src).wait_recv()
            total = total + zrecv[a, src].astype(F32)
        gw_ref[:, a, :] = total

    for k in range(1, n):
        forward(peer(k)).wait_send()
        back_to(source(k)).wait_send()
    for a in range(2):
        for k in range(x_n):
            to_core(a, (xx + k) % x_n).wait_send()
        for k in range(1, x_n):
            to_x_copy(a, (xx + k) % x_n).wait_send()
        for k in range(1, zl_n):
            to_z_copy(a, (zl + k) % zl_n).wait_send()


def on_device(dims, tokens, cotangent, gates, expert_ids, slot_ids, w_in, w_out):
    zh_n, y_n, x_n, zl_n, c_n = dims
    n = zh_n * y_n
    rows, width = tokens.shape
    ff = w_in.shape[2]
    scale = 1.0 / math.sqrt(n * x_n * zl_n * c_n * CAP)
    per = 10 * n
    near = n - y_n
    near_rows, far_rows = round_up(10 * near), round_up(10 * y_n)
    dma = pltpu.SemaphoreType.DMA
    hbm = pl.BlockSpec(memory_space=pltpu.HBM)
    vmem = pl.BlockSpec(memory_space=pltpu.VMEM)
    return pl.pallas_call(
        functools.partial(kernel, dims, scale),
        out_shape=(
            jax.ShapeDtypeStruct((rows, width), BF16),
            jax.ShapeDtypeStruct((ff // (x_n * zl_n * c_n), 2, width), F32),
        ),
        in_specs=[hbm] * 7,
        out_specs=(vmem, vmem),
        scratch_shapes=[
            pltpu.VMEM((rows, width), BF16),
            pltpu.VMEM((rows, width), BF16),
            pltpu.VMEM((1, rows), F32),
            pltpu.VMEM((1, rows), jnp.int32),
            pltpu.VMEM((1, rows), jnp.int32),
            pltpu.VMEM(w_in.shape, BF16),
            pltpu.VMEM(w_out.shape, BF16),
            pltpu.VMEM((n, 16, 2 * width + width // 2), BF16),
            pltpu.VMEM((n, 16, 2 * width + width // 2), BF16),
            pltpu.VMEM((2, near_rows, 2 * width), F32),
            pltpu.VMEM((2, far_rows, 2 * width), F32),
            pltpu.VMEM((16 * max(near, y_n), width // 2), BF16),
            pltpu.VMEM((2, near_rows, width), F32),
            pltpu.VMEM((2, far_rows, width), F32),
            pltpu.VMEM((n, 16, width + width // 4), BF16),
            pltpu.VMEM((n, 16, width + width // 4), BF16),
            pltpu.VMEM((2, x_n, zl_n, c_n, 16, width), F32),
            pltpu.VMEM((2, x_n, zl_n, 16, width), F32),
            pltpu.VMEM((2, x_n, zl_n, 16, width), BF16),
            pltpu.VMEM((2, x_n, zl_n, 16, width), BF16),
            pltpu.VMEM((2, x_n, zl_n, 16, width), BF16),
            pltpu.VMEM((2, x_n, zl_n, 16, width), BF16),
            pltpu.VMEM((2, zl_n, 16, width), BF16),
            pltpu.VMEM((2, zl_n, 16, width), BF16),
            dma((5,)),
            dma((2,)),
            dma((n,)),
            dma((n,)),
            dma((n,)),
            dma((n,)),
            dma((2, x_n)),
            dma((2, x_n)),
            dma((2, x_n)),
            dma((2, x_n)),
            dma((2, zl_n)),
            dma((2, zl_n)),
        ],
        compiler_params=pltpu.CompilerParams(
            collective_id=0, has_side_effects=True, vmem_limit_bytes=48 << 20
        ),
        cost_estimate=pl.CostEstimate(
            flops=8 * 2 * per * width * ff, bytes_accessed=6 << 20, transcendentals=2 * per * ff
        ),
        name="expert_backward",
    )(
        tokens, cotangent, gates.reshape(1, rows), expert_ids.reshape(1, rows),
        slot_ids.reshape(1, rows), w_in, w_out,
    )


def solution(mesh, dims=(ZH, Y, X, ZL, C)):
    return jax.shard_map(
        functools.partial(on_device, dims),
        mesh=mesh,
        in_specs=(
            P(("expert", "dp"), None),
            P(("expert", "dp"), None),
            P(("expert", "dp")),
            P(("expert", "dp")),
            P(("expert", "dp")),
            P("expert", None, None),
            P("expert", None, None),
        ),
        out_specs=(P(("expert", "dp"), None), P("dp", "expert", None)),
        check_vma=False,
    )
```

time: 141 us -> 140 us (level)
  no operation moved by 1% of the time
where the time goes in v2:
time: 140 us
  Pallas kernels  131 us (94%)
  local copies, waits for them, and re-layouts  8.44 us (6%)
    pallas_call x1, Pallas kernels, on_device(): pl.pallas_call(functools.partial(kernel, dims, scale), out_shape=(jax.Sha...  131 us
    unnamed x16, local copies, waits for them, and re-layouts  8.44 us

profile of v2, /device:TPU:1, one launch (start us, length us, event | category | flops | bytes accessed | tf_op | source)
XLA Modules:
  0.0 139.9 jit_solution(15461714305872466439)
XLA Ops:
  0.6 0.0 copy-start
  0.6 1.6 %copy-done = bf16[2,512,1024]{2,1,0:T(8,128)(2,1)S(1)} copy-done((bf16[2,512,1024]{2,1,0:T(8,128)(2,1)S(1)}, bf16[2,512,1024]{2,1,0:T(8,128)(2,1)}, u32[]{:S(2)}) %copy-start) | copy-done | bytes 2097176
  2.2 0.0 copy-start.1
  2.2 1.6 %copy-done.1 = bf16[2,1024,512]{2,1,0:T(8,128)(2,1)S(1)} copy-done((bf16[2,1024,512]{2,1,0:T(8,128)(2,1)S(1)}, bf16[2,1024,512]{2,1,0:T(8,128)(2,1)}, u32[]{:S(2)}) %copy-start.1) | copy-done | bytes 2097176
  3.8 0.0 copy-start.2
  3.8 0.9 copy-done.2
  4.8 0.0 copy-start.3
  4.8 0.9 copy-done.3
  5.7 0.0 copy-start.4
  5.7 0.7 copy-done.4
  6.4 0.0 copy-start.5
  6.4 0.7 copy-done.5
  7.1 0.0 copy-start.6
  7.1 0.7 copy-done.6
  7.8 130.8 %expert_backward.1 = (bf16[256,512]{1,0:T(8,128)(2,1)S(1)}, f32[16,2,512]{2,1,0:T(2,128)S(1)}) custom-call(bf16[256,512]{1,0:T(8,128)(2,1)S(1)} %copy-done.2, bf16[256,512]{1,0:T(8,128)(2,1)S(1)} %copy-done.3, f32[1,256]{1,0:T(1,128)S(1)} %bitcast.3, s32[1,256]{1,0:T(1,128)S(1)} %bitcast.4, s32[1,256]{1,0:T(1,128)S(1)} %bitcast.5, ...), custom_call_target="tpu_custom_call" | custom-call | flops 1342177280 | bytes 6291456 | tf_op jit(solution)/shard_map/expert_backward/pallas_call | solution.py:370
  138.6 0.7 copy.11
  139.3 0.6 copy.12
Async XLA Ops:
  0.6 1.6 %copy-start = (bf16[2,512,1024]{2,1,0:T(8,128)(2,1)S(1)}, bf16[2,512,1024]{2,1,0:T(8,128)(2,1)}, u32[]{:S(2)}) copy-start(bf16[2,512,1024]{2,1,0:T(8,128)(2,1)} %win_hbm.1) | copy-start | bytes 6291460
  2.2 1.6 %copy-start.1 = (bf16[2,1024,512]{2,1,0:T(8,128)(2,1)S(1)}, bf16[2,1024,512]{2,1,0:T(8,128)(2,1)}, u32[]{:S(2)}) copy-start(bf16[2,1024,512]{2,1,0:T(8,128)(2,1)} %wout_hbm.1) | copy-start | bytes 6291460
  3.8 0.9 copy-start.2
  4.8 0.9 copy-start.3
  5.7 0.7 copy-start.4
  6.4 0.7 copy-start.5
  7.1 0.7 copy-start.6

commit v3 on v2

--- a/solution.py
+++ b/solution.py
@@ -414,7 +414,7 @@
             dma((2, zl_n)),
         ],
         compiler_params=pltpu.CompilerParams(
-            collective_id=0, has_side_effects=True, vmem_limit_bytes=48 << 20
+            collective_id=0, has_side_effects=True, vmem_limit_bytes=60 << 20
         ),
         cost_estimate=pl.CostEstimate(
             flops=8 * 2 * per * width * ff, bytes_accessed=6 << 20, transcendentals=2 * per * ff

time: 140 us -> 135 us (0.964)
  local copies, waits for them, and re-layouts: 8.44 us -> 3.14 us
    unnamed x16 -> x2, local copies, waits for them, and re-layouts: 8.44 us -> 3.14 us
where the time goes in v3:
time: 135 us
  Pallas kernels  131 us (97%)
  local copies, waits for them, and re-layouts  3.14 us (2%)
    pallas_call x1, Pallas kernels, on_device(): pl.pallas_call(functools.partial(kernel, dims, scale), out_shape=(jax.Sha...  131 us
    unnamed x2, local copies, waits for them, and re-layouts  3.14 us

profile of v3, /device:TPU:1, one launch (start us, length us, event | category | flops | bytes accessed | tf_op | source)
XLA Modules:
  0.0 135.0 jit_solution(2227299044346940127)
XLA Ops:
  0.6 131.2 %expert_backward.1 = (bf16[256,512]{1,0:T(8,128)(2,1)}, f32[16,2,512]{2,1,0:T(2,128)}) custom-call(bf16[256,512]{1,0:T(8,128)(2,1)} %tok_hbm.1, bf16[256,512]{1,0:T(8,128)(2,1)} %cot_hbm.1, f32[1,256]{1,0:T(1,128)} %bitcast.3, s32[1,256]{1,0:T(1,128)} %bitcast.4, s32[1,256]{1,0:T(1,128)} %bitcast.5, bf16[2,512,1024]{2,1,0:T(8,128)(2,1)} %win_hbm.1, ...), custom_call_target="tpu_custom_call" | custom-call | flops 1342177280 | bytes 6291456 | tf_op jit(solution)/shard_map/expert_backward/pallas_call | solution.py:370
  131.9 1.7 %copy.11 = bf16[256,512]{1,0:T(8,128)(2,1)} copy(bf16[256,512]{1,0:T(8,128)(2,1)} %get-tuple-element.4) | data formatting | bytes 524288
  133.5 1.5 %copy.12 = f32[16,2,512]{2,1,0:T(2,128)} copy(f32[16,2,512]{2,1,0:T(2,128)} %get-tuple-element.5) | data formatting | bytes 131072

commit v4 on v3

v4 whole, which is shorter than its diff:
```python
import functools
import math

import jax
import jax.numpy as jnp
from jax import lax
from jax.experimental import pallas as pl
from jax.experimental.pallas import tpu as pltpu
from jax.sharding import PartitionSpec as P

MESH = pl.DeviceIdType.MESH
CAP = 10
F32 = jnp.float32
BF16 = jnp.bfloat16
ZH, Y, X, ZL, C = 4, 4, 4, 8, 2


def nn(a, b):
    return lax.dot_general(a, b, (((1,), (0,)), ((), ())), preferred_element_type=F32)


def nt(a, b):
    return lax.dot_general(a, b, (((1,), (1,)), ((), ())), preferred_element_type=F32)


def tn(a, b):
    return lax.dot_general(a, b, (((0,), (0,)), ((), ())), preferred_element_type=F32)


def one_hot(rows, cols):
    return jnp.where(rows == cols, 1.0, 0.0).astype(BF16)


def round_up(rows):
    return (rows + 15) // 16 * 16


def kernel(
    dims, scale,
    tok_hbm, cot_hbm, gate_hbm, eid_hbm, sid_hbm, win_hbm, wout_hbm,
    gt_ref, gw_ref,
    tok, cot, gate, eid, sid, win, wout, send, recv, xg_near, xg_far, tails_in, grow_near, grow_far,
    sback, rback, dsend, drecv, tsend, trecv, acc, xsend, xrecv, zsend, zrecv,
    in_sem, w_sem, fs, fr, bs, br, ds, dr, xs, xr, zs, zr,
):
    zh_n, y_n, x_n, zl_n, c_n = dims
    n = zh_n * y_n
    width = tok.shape[1]
    ff = win.shape[1]
    quarter = width // 4
    chunk = ff // x_n
    experts = c_n * n

    ex = lax.axis_index("expert")
    dp = lax.axis_index("dp")
    zh, yy = ex // y_n, ex % y_n
    xx, zl, core = dp // (zl_n * c_n), (dp // c_n) % zl_n, dp % c_n
    other = 1 - core
    here = ex * c_n + core

    steps_z = sorted(range(zh_n), key=lambda dz: min(dz, zh_n - dz))
    offsets = [(dz, dy) for dz in steps_z for dy in range(y_n)]
    near = n - y_n

    def peer(k):
        dz, dy = offsets[k]
        return ((zh + dz) % zh_n) * y_n + (yy + dy) % y_n

    def source(k):
        dz, dy = offsets[k]
        return ((zh + zh_n - dz) % zh_n) * y_n + (yy + y_n - dy) % y_n

    def dp_id(a, b, c):
        return (a * zl_n + b) * c_n + c

    levels = zl_n.bit_length() - 1

    def z_bit(level):
        return (zl // 2**level) % 2

    def z_partner(level):
        return zl + 2**level * (1 - 2 * z_bit(level))

    in_copies = [
        pltpu.make_async_copy(src, dst, in_sem.at[i])
        for i, (src, dst) in enumerate(
            [(eid_hbm, eid), (sid_hbm, sid), (gate_hbm, gate), (tok_hbm, tok), (cot_hbm, cot)]
        )
    ]
    w_copies = [
        pltpu.make_async_copy(win_hbm.at[core], win, w_sem.at[0]),
        pltpu.make_async_copy(wout_hbm.at[core], wout, w_sem.at[1]),
    ]
    for copy in in_copies + w_copies:
        copy.start()

    barrier = pltpu.get_barrier_semaphore()

    def greet(to_e, to_d):
        pl.semaphore_signal(barrier, inc=1, device_id=(to_e, to_d), device_id_type=MESH)

    for k in range(n):
        greet(peer(k), dp_id(xx, zl, other))
        if k > 0:
            greet(peer(k), dp)
    for k in range(1, x_n):
        greet(ex, dp_id((xx + k) % x_n, zl, core))
    for level in range(levels):
        greet(ex, dp_id(xx, z_partner(level), core))
    greet(ex, dp_id(xx, z_partner(levels - 1), other))

    for copy in in_copies[:3]:
        copy.wait()
    slot = sid[...]
    code = jnp.where(slot >= 0, eid[...] * CAP + slot, -1)
    row = lax.broadcasted_iota(jnp.int32, (8 * experts, 1), 0)
    main_code = (row // 8) * CAP + row % 8
    trow = lax.broadcasted_iota(jnp.int32, (16 * experts, 1), 0)
    tail_code = (trow // 16) * CAP + 8 + trow % 2
    t_main = one_hot(main_code, code)
    t_tail = one_hot(tail_code, code)
    gates = gate[...]
    gate_main = jnp.sum(jnp.where(main_code == code, gates, 0.0), axis=1, keepdims=True)
    gate_tail = jnp.sum(jnp.where(tail_code == code, gates, 0.0), axis=1, keepdims=True)

    for copy in in_copies[3:]:
        copy.wait()
    main_x = nn(t_main, tok[...]).reshape(experts, 8, width)
    main_g = (nn(t_main, cot[...]) * gate_main).reshape(experts, 8, width)
    send[:, :, :width] = jnp.concatenate([main_x, main_g], axis=1).astype(BF16)
    tail_x = nn(t_tail, tok[...])
    tail_g = nn(t_tail, cot[...]) * gate_tail
    block = (trow // 2) % 8
    tail = tail_x[:, :quarter]
    for q in range(1, 8):
        part = tail_x if q < 4 else tail_g
        at = (q % 4) * quarter
        tail = jnp.where(block == q, part[:, at : at + quarter], tail)
    send[:, :, width:] = tail.astype(BF16).reshape(experts, 16, quarter)

    pl.semaphore_wait(barrier, (n * c_n - 1) + (x_n - 1) + levels + 1)

    def forward(to, to_c):
        return pltpu.make_async_remote_copy(
            src_ref=send.at[to * c_n + to_c], dst_ref=recv.at[here],
            send_sem=fs.at[to * c_n + to_c], recv_sem=fr.at[here],
            device_id=(to, dp_id(xx, zl, to_c)), device_id_type=MESH,
        )

    def forward_from(src, src_c):
        at = src * c_n + src_c
        return pltpu.make_async_remote_copy(
            src_ref=send.at[at], dst_ref=recv.at[at], send_sem=fs.at[at], recv_sem=fr.at[at],
            device_id=(src, dp_id(xx, zl, src_c)), device_id_type=MESH,
        )

    def back_to(to):
        return pltpu.make_async_remote_copy(
            src_ref=sback.at[to], dst_ref=rback.at[ex], send_sem=bs.at[to], recv_sem=br.at[ex],
            device_id=(to, dp), device_id_type=MESH,
        )

    def back_from(src):
        return pltpu.make_async_remote_copy(
            src_ref=sback.at[src], dst_ref=rback.at[src], send_sem=bs.at[src], recv_sem=br.at[src],
            device_id=(src, dp), device_id_type=MESH,
        )

    def others(first, last):
        return [(k, c) for k in range(first, last) for c in ((core, other) if k else (other,))]

    for k, c in others(0, n):
        forward(peer(k), c).start()
    recv[pl.ds(here, 1)] = send[pl.ds(here, 1)]

    def gather(first, count, xg):
        total = count * c_n
        for k in range(count):
            for c in range(c_n):
                src = source(first + k) * c_n + c
                i = k * c_n + c
                rows = recv[src, :, :width].astype(F32)
                xg[i * 8 : i * 8 + 8, :width] = rows[:8]
                xg[i * 8 : i * 8 + 8, width:] = rows[8:]
                tails_in[i * 16 : i * 16 + 16, :] = recv[src, :, width:]
        part = 2 * total
        r = lax.broadcasted_iota(jnp.int32, (8 * part, 1), 0)
        col = lax.broadcasted_iota(jnp.int32, (1, 8 * part), 1)
        wanted = ((r // 2) % total) * 16 + (r // part) * 2 + r % 2
        tails = nn(one_hot(wanted, col), tails_in[: 8 * part, :])
        for q in range(8):
            xg[8 * total : 10 * total, q * quarter : (q + 1) * quarter] = tails[q * part : q * part + part]
        spare = xg.shape[0] - 10 * total
        if spare:
            xg[10 * total :, :] = jnp.zeros((spare, 2 * width), F32)

    k0 = 0.7978845608028654
    k1 = 0.044715

    def multiply(xg, grow, to_x):
        f0 = pl.multiple_of(to_x * chunk, chunk)
        xa = xg[:, :width].astype(BF16)
        ga = xg[:, width:].astype(BF16)
        w1 = win[:, pl.ds(f0, chunk)]
        w2 = wout[pl.ds(f0, chunk), :]
        pre = nn(xa, w1)
        grad_hidden = nt(ga, w2)
        square = pre * pre
        th = jnp.tanh(k0 * pre * (1.0 + k1 * square))
        cdf = 0.5 * (1.0 + th)
        hidden = (pre * cdf).astype(BF16)
        slope = cdf + 0.5 * pre * (1.0 - th * th) * (k0 * (1.0 + 3.0 * k1 * square))
        grad_pre = (grad_hidden * slope).astype(BF16)
        grow[...] += nt(grad_pre, w1)
        return tn(hidden, ga)

    def give_back(first, count, grow):
        total = count * c_n
        small = grow[8 * total : 10 * total, :].astype(BF16)
        r = lax.broadcasted_iota(jnp.int32, (16 * count, 1), 0)
        col = lax.broadcasted_iota(jnp.int32, (1, 2 * total), 1)
        spread = nn(one_hot((r // 16) * 4 + r % 4, col), small)
        picked = spread[:, :quarter]
        for q in range(1, 4):
            picked = jnp.where((r // 4) % 4 == q, spread[:, q * quarter : (q + 1) * quarter], picked)
        picked = picked.astype(BF16)
        for k in range(count):
            to = source(first + k)
            sback[to, :, :width] = grow[k * 16 : k * 16 + 16, :].astype(BF16)
            sback[to, :, width:] = picked[k * 16 : k * 16 + 16]
            if first + k > 0:
                back_to(to).start()

    for k, c in others(0, near):
        forward_from(source(k), c).wait_recv()
    gather(0, near, xg_near)
    for copy in w_copies:
        copy.wait()
    grow_near[...] = jnp.zeros_like(grow_near)
    grow_far[...] = jnp.zeros_like(grow_far)

    def near_chunk(i, carry):
        to_x = (xx + 1 + i) % x_n
        acc[to_x] = multiply(xg_near, grow_near, to_x).reshape(zl_n, c_n, 16, width)
        return carry

    lax.fori_loop(0, x_n, near_chunk, 0)
    give_back(0, near, grow_near)
    rback[pl.ds(ex, 1)] = sback[pl.ds(ex, 1)]

    def to_x_copy(to_x):
        return pltpu.make_async_remote_copy(
            src_ref=xsend.at[to_x], dst_ref=xrecv.at[xx], send_sem=xs.at[to_x], recv_sem=xr.at[xx],
            device_id=(ex, dp_id(to_x, zl, core)), device_id_type=MESH,
        )

    def from_x_copy(src):
        return pltpu.make_async_remote_copy(
            src_ref=xsend.at[src], dst_ref=xrecv.at[src], send_sem=xs.at[src], recv_sem=xr.at[src],
            device_id=(ex, dp_id(src, zl, core)), device_id_type=MESH,
        )

    def z_copy(level):
        count = zl_n >> (level + 1)
        part = pl.ds(zl_n - 2 * count, count)
        return pltpu.make_async_remote_copy(
            src_ref=zsend.at[part], dst_ref=zrecv.at[part],
            send_sem=zs.at[level], recv_sem=zr.at[level],
            device_id=(ex, dp_id(xx, z_partner(level), core)), device_id_type=MESH,
        )

    def last_copy(at, to_z, to_c, sem):
        return pltpu.make_async_remote_copy(
            src_ref=zsend.at[at, to_c], dst_ref=zrecv.at[at, core],
            send_sem=zs.at[sem], recv_sem=zr.at[sem],
            device_id=(ex, dp_id(xx, to_z, to_c)), device_id_type=MESH,
        )

    def last_from(at, src_z, src_c, sem):
        return pltpu.make_async_remote_copy(
            src_ref=zsend.at[at, src_c], dst_ref=zrecv.at[at, src_c],
            send_sem=zs.at[sem], recv_sem=zr.at[sem],
            device_id=(ex, dp_id(xx, src_z, src_c)), device_id_type=MESH,
        )

    far_z = z_partner(levels - 1)
    last = [
        (zl_n - 2, far_z, core, levels - 1),
        (zl_n - 2, far_z, other, levels),
        (zl_n - 1, zl, other, levels + 1),
    ]

    for k, c in others(near, n):
        forward_from(source(k), c).wait_recv()
    gather(near, n - near, xg_far)

    def far_chunk(i, carry):
        to_x = (xx + 1 + i) % x_n
        term = multiply(xg_far, grow_far, to_x).reshape(zl_n, c_n, 16, width)
        xsend[to_x] = ((acc[to_x] + term) * scale).astype(BF16)
        to_x_copy(to_x).start()
        return carry

    lax.fori_loop(0, x_n - 1, far_chunk, 0)
    term = multiply(xg_far, grow_far, xx).reshape(zl_n, c_n, 16, width)
    acc[xx] = (acc[xx] + term) * scale
    give_back(near, n - near, grow_far)

    for k in range(1, x_n):
        from_x_copy((xx + x_n - k) % x_n).wait_recv()
    total = acc[xx]
    for k in range(1, x_n):
        total = total + xrecv[(xx + x_n - k) % x_n].astype(F32)
    acc[xx] = total
    for level in range(levels - 1):
        count = zl_n >> (level + 1)
        at = zl_n - 2 * count
        for m in range(count):
            zsend[at + m] = acc[xx, 2 * m + 1 - z_bit(level)].astype(BF16)
        z_copy(level).start()
        z_copy(level).wait_recv()
        for m in range(count):
            acc[xx, m] = acc[xx, 2 * m + z_bit(level)] + zrecv[at + m].astype(F32)
    zsend[zl_n - 2] = acc[xx, 1 - z_bit(levels - 1)].astype(BF16)
    zsend[zl_n - 1] = acc[xx, z_bit(levels - 1)].astype(BF16)
    for where in last:
        last_copy(*where).start()

    for k in range(1, n):
        back_from(peer(k)).wait_recv()
    back = rback[:, :, :width].astype(F32)
    first, second = back[:, :8], back[:, 8:]
    mine = core == 0
    dsend[...] = jnp.where(mine, second, first).reshape(8 * n, width).astype(BF16)
    tsend[...] = rback[:, :, width:].reshape(16 * n, quarter)

    def swap(which):
        src, dst = ((dsend, drecv), (tsend, trecv))[which]
        return pltpu.make_async_remote_copy(
            src_ref=src, dst_ref=dst, send_sem=ds.at[which], recv_sem=dr.at[which],
            device_id=(ex, dp_id(xx, zl, other)), device_id_type=MESH,
        )

    for which in range(2):
        swap(which).start()
    crow = lax.broadcasted_iota(jnp.int32, (8 * n, 1), 0)
    krow = lax.broadcasted_iota(jnp.int32, (16 * n, 1), 0)

    def collect(parity, rows, tail_rows):
        codes = (2 * (crow // 8) + parity) * CAP + crow % 8
        tail_codes = jnp.where(
            (krow // 2) % 2 == core, (2 * (krow // 16) + parity) * CAP + 8 + krow % 2, -2
        )
        wide = jnp.concatenate(
            [jnp.where((krow // 4) % 4 == q, tail_rows, 0.0) for q in range(4)], axis=1
        ).astype(BF16)
        return tn(one_hot(codes, code), rows) + tn(one_hot(tail_codes, code), wide)

    kept = jnp.where(mine, first, second).reshape(8 * n, width).astype(BF16)
    result = collect(core, kept, tsend[...].astype(F32))

    for where in last:
        last_from(*where).wait_recv()
    own = acc[xx, z_bit(levels - 1), core] + zrecv[zl_n - 2, core].astype(F32)
    cross = zrecv[zl_n - 1, other].astype(F32) + zrecv[zl_n - 2, other].astype(F32)
    gw_ref[:, 0, :] = jnp.where(mine, own, cross)
    gw_ref[:, 1, :] = jnp.where(mine, cross, own)

    for which in range(2):
        swap(which).wait_recv()
    gt_ref[...] = (result + collect(other, drecv[...], trecv[...].astype(F32))).astype(BF16)

    for k, c in others(0, n):
        forward(peer(k), c).wait_send()
    for k in range(1, n):
        back_to(source(k)).wait_send()
    for which in range(2):
        swap(which).wait_send()
    for k in range(1, x_n):
        to_x_copy((xx + k) % x_n).wait_send()
    for level in range(levels - 1):
        z_copy(level).wait_send()
    for where in last:
        last_copy(*where).wait_send()


def on_device(dims, tokens, cotangent, gates, expert_ids, slot_ids, w_in, w_out):
    zh_n, y_n, x_n, zl_n, c_n = dims
    n = zh_n * y_n
    rows, width = tokens.shape
    ff = w_in.shape[2]
    scale = 1.0 / math.sqrt(n * x_n * zl_n * c_n * CAP)
    experts = c_n * n
    near = n - y_n
    near_rows, far_rows = round_up(10 * near * c_n), round_up(10 * y_n * c_n)
    dma = pltpu.SemaphoreType.DMA
    hbm = pl.BlockSpec(memory_space=pltpu.HBM)
    vmem = pl.BlockSpec(memory_space=pltpu.VMEM)
    return pl.pallas_call(
        functools.partial(kernel, dims, scale),
        out_shape=(
            jax.ShapeDtypeStruct((rows, width), BF16),
            jax.ShapeDtypeStruct((ff // (x_n * zl_n * c_n), 2, width), F32),
        ),
        in_specs=[hbm] * 7,
        out_specs=(vmem, vmem),
        scratch_shapes=[
            pltpu.VMEM((rows, width), BF16),
            pltpu.VMEM((rows, width), BF16),
            pltpu.VMEM((1, rows), F32),
            pltpu.VMEM((1, rows), jnp.int32),
            pltpu.VMEM((1, rows), jnp.int32),
            pltpu.VMEM(w_in.shape[1:], BF16),
            pltpu.VMEM(w_out.shape[1:], BF16),
            pltpu.VMEM((experts, 16, width + width // 4), BF16),
            pltpu.VMEM((experts, 16, width + width // 4), BF16),
            pltpu.VMEM((near_rows, 2 * width), F32),
            pltpu.VMEM((far_rows, 2 * width), F32),
            pltpu.VMEM((16 * c_n * max(near, y_n), width // 4), BF16),
            pltpu.VMEM((near_rows, width), F32),
            pltpu.VMEM((far_rows, width), F32),
            pltpu.VMEM((n, 16, width + width // 4), BF16),
            pltpu.VMEM((n, 16, width + width // 4), BF16),
            pltpu.VMEM((8 * n, width), BF16),
            pltpu.VMEM((8 * n, width), BF16),
            pltpu.VMEM((16 * n, width // 4), BF16),
            pltpu.VMEM((16 * n, width // 4), BF16),
            pltpu.VMEM((x_n, zl_n, c_n, 16, width), F32),
            pltpu.VMEM((x_n, zl_n, c_n, 16, width), BF16),
            pltpu.VMEM((x_n, zl_n, c_n, 16, width), BF16),
            pltpu.VMEM((zl_n, c_n, 16, width), BF16),
            pltpu.VMEM((zl_n, c_n, 16, width), BF16),
            dma((5,)),
            dma((2,)),
            dma((experts,)),
            dma((experts,)),
            dma((n,)),
            dma((n,)),
            dma((2,)),
            dma((2,)),
            dma((x_n,)),
            dma((x_n,)),
            dma((zl_n.bit_length() + 1,)),
            dma((zl_n.bit_length() + 1,)),
        ],
        compiler_params=pltpu.CompilerParams(
            collective_id=0, has_side_effects=True, vmem_limit_bytes=60 << 20
        ),
        cost_estimate=pl.CostEstimate(
            flops=8 * CAP * experts * width * ff, bytes_accessed=6 << 20, transcendentals=CAP * experts * ff
        ),
        name="expert_backward",
    )(
        tokens, cotangent, gates.reshape(1, rows), expert_ids.reshape(1, rows),
        slot_ids.reshape(1, rows), w_in, w_out,
    )


def solution(mesh, dims=(ZH, Y, X, ZL, C)):
    return jax.shard_map(
        functools.partial(on_device, dims),
        mesh=mesh,
        in_specs=(
            P(("expert", "dp"), None),
            P(("expert", "dp"), None),
            P(("expert", "dp")),
            P(("expert", "dp")),
            P(("expert", "dp")),
            P("expert", None, None),
            P("expert", None, None),
        ),
        out_specs=(P(("expert", "dp"), None), P("dp", "expert", None)),
        check_vma=False,
    )
```

time: 135 us -> 136 us (level)
  no operation moved by 1% of the time
where the time goes in v4:
time: 136 us
  Pallas kernels  132 us (97%)
  local copies, waits for them, and re-layouts  3.14 us (2%)
    pallas_call x1, Pallas kernels, on_device(): pl.pallas_call(functools.partial(kernel, dims, scale), out_shape=(jax.Sha...  132 us
    unnamed x2, local copies, waits for them, and re-layouts  3.14 us

profile of v4, /device:TPU:1, one launch (start us, length us, event | category | flops | bytes accessed | tf_op | source)
XLA Modules:
  0.0 136.0 jit_solution(9166138776943782508)
XLA Ops:
  0.6 132.3 %expert_backward.1 = (bf16[256,512]{1,0:T(8,128)(2,1)}, f32[16,2,512]{2,1,0:T(2,128)}) custom-call(bf16[256,512]{1,0:T(8,128)(2,1)} %tok_hbm.1, bf16[256,512]{1,0:T(8,128)(2,1)} %cot_hbm.1, f32[1,256]{1,0:T(1,128)} %bitcast.3, s32[1,256]{1,0:T(1,128)} %bitcast.4, s32[1,256]{1,0:T(1,128)} %bitcast.5, bf16[2,512,1024]{2,1,0:T(8,128)(2,1)} %win_hbm.1, ...), custom_call_target="tpu_custom_call" | custom-call | flops 1342177280 | bytes 6291456 | tf_op jit(solution)/shard_map/expert_backward/pallas_call | solution.py:399
  132.9 1.7 %copy.11 = bf16[256,512]{1,0:T(8,128)(2,1)} copy(bf16[256,512]{1,0:T(8,128)(2,1)} %get-tuple-element.4) | data formatting | bytes 524288
  134.6 1.5 %copy.12 = f32[16,2,512]{2,1,0:T(2,128)} copy(f32[16,2,512]{2,1,0:T(2,128)} %get-tuple-element.5) | data formatting | bytes 131072

commit v5 on v3

--- a/solution.py
+++ b/solution.py
@@ -191,7 +191,7 @@
     k1 = 0.044715
 
     def place(i):
-        return i % 2, (xx + 1 + i // 2) % x_n
+        return i // x_n, (xx + 1 + i % x_n) % x_n
 
     def multiply(xg, grow, i):
         a, to_x = place(i)
@@ -299,19 +299,25 @@
         far_chunk(i)
         return carry
 
-    def far_next(i, carry):
-        far_chunk(i)
-        a, to_x = place(i - 2)
+    def pass_x(i):
+        a, to_x = place(i)
         to_core(a, to_x).wait_recv()
         xsend[a, to_x] = (own[a, to_x] + crecv[a, to_x].astype(F32)).astype(BF16)
         to_x_copy(a, to_x).start()
+
+    def far_next(i, carry):
+        far_chunk(i)
+        pass_x(i - 2)
         return carry
 
     for k in range(near, n):
         forward_from(source(k)).wait_recv()
     gather(near, n - near, xg_far)
     lax.fori_loop(0, 2, far_first, 0)
-    lax.fori_loop(2, 2 * x_n, far_next, 0)
+    lax.fori_loop(2, x_n + 1, far_next, 0)
+    far_chunk(x_n + 1)
+    lax.fori_loop(x_n + 2, 2 * x_n, far_next, 0)
+    pass_x(2 * x_n - 2)
     give_back(near, n - near, grow_far)
 
     for a in range(2):

time: 135 us -> 136 us (level)
  no operation moved by 1% of the time
where the time goes in v5:
time: 136 us; the launch traced here: 135 us
  Pallas kernels  132 us (97%)
  local copies, waits for them, and re-layouts  3.14 us (2%)
    pallas_call x1, Pallas kernels, on_device(): pl.pallas_call(functools.partial(kernel, dims, scale), out_shape=(jax.Sha...  132 us
    unnamed x2, local copies, waits for them, and re-layouts  3.14 us

profile of v5, /device:TPU:1, one launch (start us, length us, event | category | flops | bytes accessed | tf_op | source)
XLA Modules:
  0.0 135.5 jit_solution(4569769802403848534)
XLA Ops:
  0.6 131.7 %expert_backward.1 = (bf16[256,512]{1,0:T(8,128)(2,1)}, f32[16,2,512]{2,1,0:T(2,128)}) custom-call(bf16[256,512]{1,0:T(8,128)(2,1)} %tok_hbm.1, bf16[256,512]{1,0:T(8,128)(2,1)} %cot_hbm.1, f32[1,256]{1,0:T(1,128)} %bitcast.3, s32[1,256]{1,0:T(1,128)} %bitcast.4, s32[1,256]{1,0:T(1,128)} %bitcast.5, bf16[2,512,1024]{2,1,0:T(8,128)(2,1)} %win_hbm.1, ...), custom_call_target="tpu_custom_call" | custom-call | flops 1342177280 | bytes 6291456 | tf_op jit(solution)/shard_map/expert_backward/pallas_call | solution.py:376
  132.3 1.7 %copy.11 = bf16[256,512]{1,0:T(8,128)(2,1)} copy(bf16[256,512]{1,0:T(8,128)(2,1)} %get-tuple-element.4) | data formatting | bytes 524288
  134.0 1.5 %copy.12 = f32[16,2,512]{2,1,0:T(2,128)} copy(f32[16,2,512]{2,1,0:T(2,128)} %get-tuple-element.5) | data formatting | bytes 131072

commit v6 on v3

--- a/solution.py
+++ b/solution.py
@@ -37,9 +37,9 @@
 
 def kernel(
     dims, scale,
-    tok_hbm, cot_hbm, gate_hbm, eid_hbm, sid_hbm, win_hbm, wout_hbm,
+    tok_hbm, cot_hbm, route_ref, win_hbm, wout_hbm,
     gt_ref, gw_ref,
-    tok, cot, gate, eid, sid, win, wout, send, recv, xg_near, xg_far, tails_in, grow_near, grow_far,
+    tok, cot, win, wout, send, recv, xg_near, xg_far, tails_in, grow_near, grow_far,
     sback, rback, acc, own, csend, crecv, xsend, xrecv, zsend, zrecv,
     in_sem, w_sem, fs, fr, bs, br, cs, cr, xs, xr, zs, zr,
 ):
@@ -76,7 +76,7 @@
     in_copies = [
         pltpu.make_async_copy(src, dst, in_sem.at[i])
         for i, (src, dst) in enumerate(
-            [(eid_hbm, eid), (sid_hbm, sid), (gate_hbm, gate), (tok_hbm, tok), (cot_hbm, cot)]
+            [(tok_hbm, tok), (cot_hbm, cot)]
         )
     ]
     w_copies = [
@@ -99,21 +99,19 @@
     for k in range(1, zl_n):
         greet(ex, dp_id(xx, (zl + k) % zl_n, core))
 
-    for copy in in_copies[:3]:
-        copy.wait()
-    slot = sid[...]
-    code = jnp.where(slot >= 0, eid[...] * CAP + slot, -1)
+    slot = route_ref[2:3, :].astype(jnp.int32)
+    code = jnp.where(slot >= 0, route_ref[1:2, :].astype(jnp.int32) * CAP + slot, -1)
     row = lax.broadcasted_iota(jnp.int32, (main, 1), 0)
     main_code = (row // 8) * CAP + row % 8
     tail_block = (row // 4) % 4
     tail_code = (2 * (row // 16) + (row // 2) % 2) * CAP + 8 + row % 2
     t_main = one_hot(main_code, code)
     t_tail = one_hot(tail_code, code)
-    gates = gate[...]
+    gates = route_ref[0:1, :]
     gate_main = jnp.sum(jnp.where(main_code == code, gates, 0.0), axis=1, keepdims=True)
     gate_tail = jnp.sum(jnp.where(tail_code == code, gates, 0.0), axis=1, keepdims=True)
 
-    for copy in in_copies[3:]:
+    for copy in in_copies:
         copy.wait()
     send[:, :, :width] = nn(t_main, tok[...]).astype(BF16).reshape(n, 16, width)
     send[:, :, width : 2 * width] = (
@@ -373,14 +371,11 @@
             jax.ShapeDtypeStruct((rows, width), BF16),
             jax.ShapeDtypeStruct((ff // (x_n * zl_n * c_n), 2, width), F32),
         ),
-        in_specs=[hbm] * 7,
+        in_specs=[hbm, hbm, vmem, hbm, hbm],
         out_specs=(vmem, vmem),
         scratch_shapes=[
             pltpu.VMEM((rows, width), BF16),
             pltpu.VMEM((rows, width), BF16),
-            pltpu.VMEM((1, rows), F32),
-            pltpu.VMEM((1, rows), jnp.int32),
-            pltpu.VMEM((1, rows), jnp.int32),
             pltpu.VMEM(w_in.shape, BF16),
             pltpu.VMEM(w_out.shape, BF16),
             pltpu.VMEM((n, 16, 2 * width + width // 2), BF16),
@@ -400,7 +395,7 @@
             pltpu.VMEM((2, x_n, zl_n, 16, width), BF16),
             pltpu.VMEM((2, zl_n, 16, width), BF16),
             pltpu.VMEM((2, zl_n, 16, width), BF16),
-            dma((5,)),
+            dma((2,)),
             dma((2,)),
             dma((n,)),
             dma((n,)),
@@ -414,15 +409,15 @@
             dma((2, zl_n)),
         ],
         compiler_params=pltpu.CompilerParams(
-            collective_id=0, has_side_effects=True, vmem_limit_bytes=60 << 20
+            collective_id=0, has_side_effects=True, vmem_limit_bytes=(53 << 20) + (1 << 19)
         ),
         cost_estimate=pl.CostEstimate(
             flops=8 * 2 * per * width * ff, bytes_accessed=6 << 20, transcendentals=2 * per * ff
         ),
         name="expert_backward",
     )(
-        tokens, cotangent, gates.reshape(1, rows), expert_ids.reshape(1, rows),
-        slot_ids.reshape(1, rows), w_in, w_out,
+        tokens, cotangent, jnp.stack([gates, expert_ids.astype(F32), slot_ids.astype(F32)]),
+        w_in, w_out,
     )
 
 

time: 135 us -> 135 us (level)
  other arithmetic: 0 us -> 2.05 us
  local copies, waits for them, and re-layouts: 3.14 us -> 1.33 us
    unnamed x2, local copies, waits for them, and re-layouts: 3.14 us -> 1.33 us
    convert_element_type x0 -> x2, other arithmetic: none -> 1.36 us  [the longest x1 0.68 us: on_device(): expert_ids.astype(F32)]
where the time goes in v6:
time: 135 us
  Pallas kernels  131 us (97%)
  other arithmetic  2.05 us (2%)
    pallas_call x1, Pallas kernels, on_device(): pl.pallas_call(functools.partial(kernel, dims, scale), out_shape=(jax.Sha...  131 us

profile of v6, /device:TPU:1, one launch (start us, length us, event | category | flops | bytes accessed | tf_op | source)
XLA Modules:
  0.0 135.0 jit_solution(4811094400510155845)
XLA Ops:
  0.6 0.7 convert_element_type.6
  1.3 0.7 convert_element_type.7
  2.0 0.7 pad_maximum_fusion.route_ref
  2.7 130.9 %expert_backward.1 = (bf16[256,512]{1,0:T(8,128)(2,1)S(1)}, f32[16,2,512]{2,1,0:T(2,128)S(1)}) custom-call(bf16[256,512]{1,0:T(8,128)(2,1)} %tok_hbm.1, bf16[256,512]{1,0:T(8,128)(2,1)} %cot_hbm.1, f32[3,256]{1,0:T(4,128)S(1)} %pad_maximum_fusion.route_ref, bf16[2,512,1024]{2,1,0:T(8,128)(2,1)} %win_hbm.1, bf16[2,1024,512]{2,1,0:T(8,128)(2,1)} %wout_hbm.1), custom_call_target="tpu_custom_call" | custom-call | flops 1342177280 | bytes 6291456 | tf_op jit(solution)/shard_map/expert_backward/pallas_call | solution.py:368
  133.6 0.7 copy.11
  134.3 0.6 copy.12
